TPU v7x, 256 devices: a whole 4x4x8 slice. The times are simulated.
256 devices in a mesh: rcv: 64 (over x_lo, y, z), seg: 4 (over x_hi, core).
Axes of the slice: x: 4 (x_hi: 2, x_lo: 2; x = x_hi * 2 + x_lo), y: 4, z: 8, core: 2. Of those that a mesh axis runs over, the one named last changes fastest.
Arguments:
- traces: bfloat16 [8, 8, 1024, 2048], P('seg', None, 'rcv'), may hold values from -6 to 6
- valid_flags: int32 [8], replicated, may hold values from 0 to 1, as said below
- source_block: int32 [4], replicated, may hold values from 0 to 63
Outputs:
- correlations: float32 [4, 16, 1024, 512], P(None, 'seg', 'rcv')
Inputs may be any that keep to these rules, and one draw needn't show every extreme that they name: `valid_flags`: at least one segment is valid and at least one is not.
All inputs are finite; a program needn't handle non-finite values.
Results may differ from a plain program's by a relative error of at most 0.0055.
Values may be sent and summed in bfloat16 or wider, within the bound.
A program may use at most 64 MiB of HBM per device.

v0:
```python
import math

import jax
import jax.numpy as jnp
from jax import lax
from jax.sharding import PartitionSpec as P

LAGS = 512
SB = 16
STEPS = 4


def spread(block, axis, source):
    block = jnp.where(lax.axis_index(axis) == source, block, jnp.zeros_like(block))
    return lax.psum(block, axis)


def dft_table(length):
    times = jnp.arange(length, dtype=jnp.int32)
    bins = jnp.arange(length // 2, dtype=jnp.int32)
    phase = times[:, None] * bins[None, :] % length
    angle = phase.astype(jnp.float32) * (2.0 * math.pi / length)
    return jnp.concatenate([jnp.cos(angle), -jnp.sin(angle)], axis=1).astype(jnp.bfloat16)


def lag_table(length, count):
    bins = jnp.arange(length // 2, dtype=jnp.int32)
    shifts = jnp.arange(count, dtype=jnp.int32) - count // 2 + length
    phase = bins[:, None] * shifts[None, :] % length
    angle = phase.astype(jnp.float32) * (2.0 * math.pi / length)
    return jnp.concatenate([jnp.cos(angle), -jnp.sin(angle)], axis=0)


def whiten(spectrum):
    width = spectrum.shape[-1] // 2
    real_part = spectrum[..., :width]
    imag_part = spectrum[..., width:]
    power = real_part * real_part + imag_part * imag_part
    level = 0.25 * jnp.mean(power, axis=-1, keepdims=True) + 1e-06
    factor = 1.0 / jnp.sqrt(power + level)
    return (spectrum * jnp.concatenate([factor, factor], axis=-1)).astype(jnp.bfloat16)


def cross(sources, receivers):
    width = sources.shape[-1] // 2
    src_rows = sources.reshape(-1, sources.shape[-2], sources.shape[-1])
    rcv_rows = receivers.reshape(-1, receivers.shape[-2], receivers.shape[-1])
    total_rows = src_rows.shape[0]

    def add_row(index, totals):
        real_acc, imag_acc = totals
        src_one = lax.dynamic_index_in_dim(src_rows, index, 0, False).astype(jnp.float32)
        rcv_one = lax.dynamic_index_in_dim(rcv_rows, index, 0, False).astype(jnp.float32)
        s_real = src_one[:, None, :width]
        s_imag = src_one[:, None, width:]
        r_real = rcv_one[None, :, :width]
        r_imag = rcv_one[None, :, width:]
        real_acc = real_acc + (s_real * r_real + s_imag * r_imag)
        imag_acc = imag_acc + (s_real * r_imag - s_imag * r_real)
        return (real_acc, imag_acc)

    zeros = jnp.zeros((src_rows.shape[1], rcv_rows.shape[1], width), jnp.float32)
    real_sum, imag_sum = lax.fori_loop(0, total_rows, add_row, (zeros, zeros))
    return jnp.concatenate([real_sum, imag_sum], axis=-1)


def local(traces, valid_flags, source_block):
    seg_local, frames, rcv_local, length = traces.shape
    block_width = SB
    table = dft_table(length)
    lagtab = lag_table(length, LAGS)

    def spectra(segment):
        flat = segment.reshape(-1, length)
        return whiten(jnp.dot(flat, table, preferred_element_type=jnp.float32)).reshape(
            frames, rcv_local, length
        )

    whitened = lax.map(spectra, traces)
    seg_start = lax.axis_index("seg") * seg_local
    own_flags = lax.dynamic_slice_in_dim(valid_flags, seg_start, seg_local, 0)
    masked = whitened * own_flags.astype(jnp.bfloat16)[:, None, None, None]
    count = frames * jnp.sum(valid_flags)
    denom = jnp.sqrt(jnp.float32(length // 2) * count.astype(jnp.float32))
    blocks_here = rcv_local // block_width
    results = []
    for number in range(STEPS):
        chosen = source_block[number]
        holder = chosen // blocks_here
        sources = spread(whitened, "rcv", holder)
        rounded = cross(sources, masked).astype(jnp.bfloat16)
        grouped = rounded.reshape(block_width, 1, rcv_local, length)
        received = lax.all_to_all(grouped, "seg", split_axis=0, concat_axis=1, tiled=True)
        stack = jnp.sum(received.astype(jnp.float32), axis=1)
        kept = stack.shape[0]
        lagged = jnp.dot(
            stack.reshape(-1, length),
            lagtab,
            precision=lax.Precision.HIGHEST,
            preferred_element_type=jnp.float32,
        )
        lagged = lagged.reshape(kept, rcv_local, LAGS)
        results.append(lagged / denom)
    return jnp.stack(results)


def solution(mesh):
    placed = (P("seg", None, "rcv", None), P(), P())
    return jax.shard_map(
        local, mesh=mesh, in_specs=placed, out_specs=P(None, "seg", "rcv", None), check_vma=False
    )
```

profile of v0, /device:TPU:1, one launch (start us, length us, event | category | flops | bytes accessed | tf_op | source)
XLA Modules:
  0.0 1040.3 jit_solution(3804861718175667403)
XLA Ops:
  6.5 35.0 %negate_convert_fusion = (bf16[2048,1024]{1,0:T(8,128)(2,1)}, bf16[2048,1024]{1,0:T(8,128)(2,1)}) fusion(), kind=kLoop, calls=%fused_computation.33 | loop fusion | flops 35651584 | bytes 8388608 | tf_op jit(solution)/shard_map/convert.29
  44.8 8.3 pad_maximum_fusion
  53.0 12.0 %while.81 = (s32[]{:T(128)}, bf16[2,8,16,2048]{3,2,1,0:T(8,128)(2,1)}, bf16[2,8,16,2048]{3,2,1,0:T(8,128)(2,1)S(1)}, bf16[2048,2048]{1,0:T(8,128)(2,1)}) while((s32[]{:T(128)}, bf16[2,8,16,2048]{3,2,1,0:T(8,128)(2,1)}, bf16[2,8,16,2048]{3,2,1,0:T(8,128)(2,1)S(1)}, bf16[2048,2048]{1,0:T(8,128)(2,1)}) %tuple.240), condition=%wide.region_2.3_spmd.clone, body=%wide.region_0.2_spmd.sunk.clone | while | flops 1075576960 | bytes 16779832 | solution.py:79
  53.1 4.6 fusion.76
  59.1 4.6 fusion.76
  65.2 3.6 broadcast_multiply_fusion
  70.1 9.2 fusion.27
  79.3 565.6 %all-reduce.3.cloned.1.call-done = (bf16[16,16,2048]{2,1,0:T(8,128)(2,1)}, bf16[16,16,2048]{2,1,0:T(8,128)(2,1)}, bf16[16,16,2048]{2,1,0:T(8,128)(2,1)}, bf16[16,16,2048]{2,1,0:T(8,128)(2,1)}) async-done(((bf16[16,16,2048]{2,1,0:T(8,128)(2,1)}, bf16[16,16,2048]{2,1,0:T(8,128)(2,1)}, bf16[16,16,2048]{2,1,0:T(8,128)(2,1)}, bf16[16,16,2048]{2,1,0:T(8,128)(2,1)}), (bf16[16,16,2048]{2,1,0:T(8,128)(2,1)}, ...) | async-done | bytes 4194320 | tf_op jit(solution)/shard_map/psum | solution.py:15
  645.0 67.3 %while.82 = (s32[]{:T(128)}, f32[16,16,1024]{2,1,0:T(8,128)}, f32[16,16,1024]{2,1,0:T(8,128)}, bf16[16,16,2048]{2,1,0:T(8,128)(2,1)}, bf16[16,16,2048]{2,1,0:T(8,128)(2,1)}) while((s32[]{:T(128)}, f32[16,16,1024]{2,1,0:T(8,128)}, f32[16,16,1024]{2,1,0:T(8,128)}, bf16[16,16,2048]{2,1,0:T(8,128)(2,1)}, ...), condition=%wide.region_5.6_spmd.clone.clone, body=%wide.region_4.5_spmd.clone.sunk.clone | while | flops 2686979 | bytes 5374027 | solution.py:63
  715.0 50.9 %all-to-all-start = ((bf16[16,1,16,2048]{3,2,1,0:T(8,128)(2,1)}), bf16[16,1,16,2048]{3,2,1,0:T(8,128)(2,1)}, u32[]{:S(2)}, u32[]{:S(2)}) async-start(bf16[16,1,16,2048]{3,2,1,0:T(8,128)(2,1)} %pad_maximum_fusion.1), calls=%async_computation | async-start | bytes 2097152 | tf_op jit(solution)/shard_map/all_to_all | solution.py:93
  765.9 68.9 %while.83 = (s32[]{:T(128)}, f32[16,16,1024]{2,1,0:T(8,128)}, f32[16,16,1024]{2,1,0:T(8,128)}, bf16[16,16,2048]{2,1,0:T(8,128)(2,1)}, bf16[16,16,2048]{2,1,0:T(8,128)(2,1)}) while((s32[]{:T(128)}, f32[16,16,1024]{2,1,0:T(8,128)}, f32[16,16,1024]{2,1,0:T(8,128)}, bf16[16,16,2048]{2,1,0:T(8,128)(2,1)}, ...), condition=%wide.region_10.11_spmd.clone.clone, body=%wide.region_9.10_spmd.clone.sunk.clone | while | flops 2686979 | bytes 5374027 | solution.py:63
  774.1 3.5 select_add_fusion.17
  787.3 3.5 select_add_fusion.17
  822.5 3.5 select_add_fusion.17
  834.8 68.7 %while.84 = (s32[]{:T(128)}, f32[16,16,1024]{2,1,0:T(8,128)}, f32[16,16,1024]{2,1,0:T(8,128)}, bf16[16,16,2048]{2,1,0:T(8,128)(2,1)}, bf16[16,16,2048]{2,1,0:T(8,128)(2,1)}) while((s32[]{:T(128)}, f32[16,16,1024]{2,1,0:T(8,128)}, f32[16,16,1024]{2,1,0:T(8,128)}, bf16[16,16,2048]{2,1,0:T(8,128)(2,1)}, ...), condition=%wide.region_14.15_spmd.clone.clone, body=%wide.region_13.14_spmd.clone.sunk.clone | while | flops 2686979 | bytes 5374027 | solution.py:63
  903.5 62.3 %while.85 = (s32[]{:T(128)}, f32[16,16,1024]{2,1,0:T(8,128)S(1)}, f32[16,16,1024]{2,1,0:T(8,128)}, bf16[16,16,2048]{2,1,0:T(8,128)(2,1)}, bf16[16,16,2048]{2,1,0:T(8,128)(2,1)}) while((s32[]{:T(128)}, f32[16,16,1024]{2,1,0:T(8,128)S(1)}, f32[16,16,1024]{2,1,0:T(8,128)}, bf16[16,16,2048]{2,1,0:T(8,128)(2,1)}, ...), condition=%wide.region_18.19_spmd.clone.clone, body=%wide.region_17.18_spmd.clone.sunk.clone | while | flops 2686979 | bytes 5374027 | solution.py:63
  968.5 4.8 all-to-all-start.1
  976.8 11.6 %all-to-all-done.1 = bf16[16,1,16,2048]{3,2,1,0:T(8,128)(2,1)} async-done(((bf16[16,1,16,2048]{3,2,1,0:T(8,128)(2,1)}), bf16[16,1,16,2048]{3,2,1,0:T(8,128)(2,1)}, u32[]{:S(2)}, u32[]{:S(2)}) %all-to-all-start.1) | async-done | bytes 1048608 | tf_op jit(solution)/shard_map/all_to_all | solution.py:93
  988.5 5.1 all-to-all-start.2
  1000.2 8.6 all-to-all-done.2
  1008.8 4.4 all-to-all-start.3
  1014.6 4.5 fusion.20
  1024.4 3.8 all-to-all-done.3
  1028.4 4.2 fusion.26
  (318 shorter events, 282.6 us)
Async XLA Ops:
  6.5 638.4 %all-reduce.3.cloned.1.call-start = ((), (), s32[]{:S(2)}) async-start(), calls=%async_computation.4 | async-start | bytes 8388608 | tf_op jit(solution)/shard_map/psum | solution.py:15
  6.5 35.0 %copy-start.7 = (s32[4]{0:T(128)S(1)}, s32[4]{0:T(128)}, u32[]{:S(2)}) copy-start(s32[4]{0:T(128)} %param.15) | copy-start | bytes 52
  44.8 8.3 copy-start.5
  53.0 12.1 %copy-start.8 = (s32[8]{0:T(128)S(1)}, s32[8]{0:T(128)}, u32[]{:S(2)}) copy-start(s32[8]{0:T(128)} %param.14) | copy-start | bytes 100
  712.3 1.5 copy-start.4
  715.0 253.5 %all-to-all-start = ((bf16[16,1,16,2048]{3,2,1,0:T(8,128)(2,1)}), bf16[16,1,16,2048]{3,2,1,0:T(8,128)(2,1)}, u32[]{:S(2)}, u32[]{:S(2)}) async-start(bf16[16,1,16,2048]{3,2,1,0:T(8,128)(2,1)} %pad_maximum_fusion.1), calls=%async_computation | async-start | bytes 2097152 | tf_op jit(solution)/shard_map/all_to_all | solution.py:93
  965.8 1.5 copy-start.3
  968.5 20.0 %all-to-all-start.1 = ((bf16[16,1,16,2048]{3,2,1,0:T(8,128)(2,1)}), bf16[16,1,16,2048]{3,2,1,0:T(8,128)(2,1)}, u32[]{:S(2)}, u32[]{:S(2)}) async-start(bf16[16,1,16,2048]{3,2,1,0:T(8,128)(2,1)} %pad_maximum_fusion.2), calls=%async_computation.1 | async-start | bytes 2097152 | tf_op jit(solution)/shard_map/all_to_all | solution.py:93
  973.3 1.5 copy-start.2
  974.7 1.3 copy-start.1
  988.5 20.3 %all-to-all-start.2 = ((bf16[16,1,16,2048]{3,2,1,0:T(8,128)(2,1)}), bf16[16,1,16,2048]{3,2,1,0:T(8,128)(2,1)}, u32[]{:S(2)}, u32[]{:S(2)}) async-start(bf16[16,1,16,2048]{3,2,1,0:T(8,128)(2,1)} %pad_maximum_fusion.3), calls=%async_computation.2 | async-start | bytes 2097152 | tf_op jit(solution)/shard_map/all_to_all | solution.py:93
  1008.8 19.5 %all-to-all-start.3 = ((bf16[16,1,16,2048]{3,2,1,0:T(8,128)(2,1)}), bf16[16,1,16,2048]{3,2,1,0:T(8,128)(2,1)S(1)}, u32[]{:S(2)}, u32[]{:S(2)}) async-start(bf16[16,1,16,2048]{3,2,1,0:T(8,128)(2,1)} %pad_maximum_fusion.4), calls=%async_computation.3 | async-start | bytes 2097152 | tf_op jit(solution)/shard_map/all_to_all | solution.py:93
  1014.6 4.6 copy-start
  1014.6 4.6 copy-start.6
Sparse Core Ops, SparseCore 0:
  68.9 576.0 all-reduce.2
where the time goes:
time: 1050 us; the launch traced here: 1040 us
  waiting for transfers between devices  590 us (56%)
  other arithmetic  339 us (32%)
  starting transfers between devices  65.2 us (6%)
  matrix products  23.3 us (2%)
  between operations  16.8 us (2%)
    psum x1, waiting for transfers between devices, spread(): return lax.psum(block, axis)  566 us
    add x64, other arithmetic, add_row(): imag_acc = imag_acc + (s_real * r_imag - s_imag * r_real)  207 us
    all_to_all x4, starting transfers between devices, local(): lax.all_to_all(grouped, 'seg', split_axis=0, concat_axis=1, tiled=True)  65.2 us
    convert_element_type x64, other arithmetic, add_row(): lax.dynamic_index_in_dim(rcv_rows, index, 0, False).astype(jnp.float32)  56.9 us
    another operation x2, other arithmetic  35 us
    all_to_all x4, waiting for transfers between devices, local(): lax.all_to_all(grouped, 'seg', split_axis=0, concat_axis=1, tiled=True)  24 us
  transfers between devices with their start and end apart: 5, of which 4 were waited for; matrix products, arithmetic and copies ran while one was open for 22% of the time, Pallas kernels for 0%

commit v1 on v0

v1 whole, which is shorter than its diff:
```python
import math

import jax
import jax.numpy as jnp
import ml_dtypes
import numpy as np
from jax import lax
from jax.experimental import pallas as pl
from jax.experimental.pallas import tpu as pltpu
from jax.sharding import PartitionSpec as P

MESH = pl.DeviceIdType.MESH
NFFT = 2048
HALF = NFFT // 2
LAGS = 512
SB = 16
STEPS = 4
NY, NZ = 4, 8
KQ = 4
QB = HALF // KQ
QL = 2 * QB
F32, BF16 = jnp.float32, jnp.bfloat16


def dft_table():
    t = np.arange(NFFT)[:, None]
    k = np.arange(HALF)[None, :]
    angle = ((t * k) % NFFT) * (2.0 * math.pi / NFFT)
    both = np.stack([np.cos(angle), -np.sin(angle)], 1).reshape(NFFT, 2, KQ, QB)
    return both.transpose(2, 0, 1, 3).reshape(KQ, NFFT, QL).astype(ml_dtypes.bfloat16)


def lag_table():
    k = np.arange(HALF)[:, None]
    tau = np.arange(LAGS)[None, :] - LAGS // 2 + NFFT
    angle = ((k * tau) % NFFT) * (2.0 * math.pi / NFFT)
    full = np.concatenate([np.cos(angle), -np.sin(angle)], 0).astype(np.float32)
    high = full.astype(ml_dtypes.bfloat16)
    low = (full - high.astype(np.float32)).astype(ml_dtypes.bfloat16)
    parts = [a[:, h * 256 : h * 256 + 256] for a in (high, low) for h in (0, 1)]
    return np.stack(parts)


def kernel(
    x_ref, flags, blocks, tab_hbm, lag_hbm, out,
    tab, lag, spec, w, rb1, rp, cand, rb20, rb21, rb22, rb23, src, r3, s3, z, lf,
    send_c, recv_c, send_x, recv_x, send_h, recv_h, own_c, own_x, own_h,
    tab_sem, a1_s, a1_r, rx_sem, az_s, az_r, gz_s, gz_r, gy_s, gy_r, rs_s, rs_r,
):
    rb2 = (rb20, rb21, rb22, rb23)
    rcv, seg = lax.axis_index("rcv"), lax.axis_index("seg")
    px, py, pz = rcv // 32, (rcv // 8) % 4, rcv % 8
    ph, pc = seg // 2, seg % 2
    me_q = px * NY + py

    def at_xy(dx, dy):
        return (px + dx) % 2, (py + dy) % NY

    def dev_xy(dx, dy):
        tx, ty = at_xy(dx, dy)
        return (tx * 32 + ty * 8 + pz, seg)

    def dev_z(dz):
        return (px * 32 + py * 8 + (pz + dz) % NZ, seg)

    dev_c = (rcv, ph * 2 + 1 - pc)
    dev_h = (rcv, (1 - ph) * 2 + pc)
    plane = [(dx, dy) for dx in (0, 1) for dy in range(NY) if dx or dy]

    barrier = pltpu.get_barrier_semaphore()
    peers = [dev_xy(*d) for d in plane] + [dev_z(d) for d in range(1, NZ)] + [dev_c, dev_h]
    for peer in peers:
        pl.semaphore_signal(barrier, inc=1, device_id=peer, device_id_type=MESH)

    loads = [pltpu.make_async_copy(tab_hbm.at[q], tab.at[q], tab_sem.at[q]) for q in range(KQ)]
    loads.append(pltpu.make_async_copy(lag_hbm, lag, tab_sem.at[KQ]))
    for load in loads:
        load.start()

    def remote(a, b, s, r, peer):
        return pltpu.make_async_remote_copy(
            src_ref=a, dst_ref=b, send_sem=s, recv_sem=r, device_id=peer, device_id_type=MESH
        )

    rows = x_ref[...].reshape(256, NFFT)
    for q in range(KQ):
        loads[q].wait()
        spec[q] = jnp.dot(rows, tab[q], preferred_element_type=F32)

    def whiten(row, _):
        at = pl.ds(pl.multiple_of(row * SB, SB), SB)
        parts = [spec[q, at, :] for q in range(KQ)]
        powers = [p[:, :QB] * p[:, :QB] + p[:, QB:] * p[:, QB:] for p in parts]
        total = sum(jnp.sum(p, axis=-1, keepdims=True) for p in powers)
        level = 0.25 * (total * (1.0 / HALF)) + 1e-06
        for q in range(KQ):
            factor = lax.rsqrt(powers[q] + level)
            w[row // 8, q, row % 8] = (parts[q] * jnp.concatenate([factor, factor], -1)).astype(BF16)
        return 0

    lax.fori_loop(0, 16, whiten, 0)

    pl.semaphore_wait(barrier, len(peers))

    sent = []
    first = []
    for i, (dx, dy) in enumerate(plane):
        tx, ty = at_xy(dx, dy)
        copy = remote(w.at[tx, ty], rb1.at[me_q], a1_s.at[i], a1_r.at[i], dev_xy(dx, dy))
        copy.start()
        first.append(copy)
    swap = remote(w.at[1 - px], rp, rx_sem.at[0], rx_sem.at[1], dev_xy(1, 0))
    swap.start()
    sent += first + [swap]
    rb1[me_q] = w[px, py]

    def fill(ref, row):
        def one(f, _):
            for q in range(KQ):
                re = ref[q, f, :, :QB].astype(F32)
                im = ref[q, f, :, QB:].astype(F32)
                at = (f, pl.ds(pl.multiple_of(row * SB, SB), SB), pl.ds(q * QB, QB))
                r3[(0,) + at] = re
                r3[(1,) + at] = im
                r3[(2,) + at] = re + im
            return 0

        lax.fori_loop(0, NZ, one, 0)

    fill(w.at[px], px)
    for copy in first:
        copy.wait_recv()
    across = []
    for s in range(STEPS):
        chosen = rb1[blocks[s] // NZ]
        cand[:, s] = chosen
        rb2[s][pz] = cand[pz, s]
        group = []
        for dz in range(1, NZ):
            copy = remote(cand.at[(pz + dz) % NZ, s], rb2[s].at[pz], az_s.at[s, dz], az_r.at[s, dz], dev_z(dz))
            copy.start()
            group.append(copy)
        across.append(group)
        sent += group
    along = []
    for s in range(STEPS):
        for copy in across[s]:
            copy.wait_recv()
        src[s, py, pz] = rb2[s][blocks[s] % NZ]
        group = []
        for dz in range(1, NZ):
            here = src.at[s, py, pz]
            copy = remote(here, here, gz_s.at[s, dz], gz_r.at[s, dz], dev_z(dz))
            copy.start()
            group.append(copy)
        along.append(group)
        sent += group
    over = []
    for s in range(STEPS):
        for copy in along[s]:
            copy.wait_recv()
        group = []
        for dy in (1, 3, 2):
            here = src.at[s, py]
            copy = remote(here, here, gy_s.at[s, dy], gy_r.at[s, dy], dev_xy(0, dy))
            copy.start()
            group.append(copy)
        over.append(group)
        sent += group
    swap.wait_recv()
    fill(rp, 1 - px)
    loads[KQ].wait()

    count = flags[0]
    for g in range(1, 8):
        count = count + flags[g]
    scale = 1.0 / jnp.sqrt(jnp.full((SB, LAGS), HALF, F32) * (8 * count).astype(F32))
    keep = flags[seg * 2 + px].astype(F32)

    stage_c, stage_x, stage_h = [], [], []

    def to_x(s):
        stage_c[s].wait_recv()

        def one(b, _):
            for xc in range(2):
                own_c[b, xc] = own_c[b, xc] + recv_c[s, b // 4, b % 4, xc].astype(F32)
            send_x[s, b // 4, b % 4] = own_c[b, 1 - px].astype(BF16)
            own_x[s, b // 4, b % 4] = own_c[b, px]
            return 0

        lax.fori_loop(0, 8, one, 0)
        copy = remote(send_x.at[s], recv_x.at[s], rs_s.at[1, s], rs_r.at[1, s], dev_xy(1, 0))
        copy.start()
        stage_x.append(copy)
        sent.append(copy)

    def to_h(s):
        stage_x[s].wait_recv()
        for jj in range(4):
            send_h[s, jj] = (own_x[s, 1 - ph, jj] + recv_x[s, 1 - ph, jj].astype(F32)).astype(BF16)
            own_h[s, jj] = own_x[s, ph, jj] + recv_x[s, ph, jj].astype(F32)
        copy = remote(send_h.at[s], recv_h.at[s], rs_s.at[2, s], rs_r.at[2, s], dev_h)
        copy.start()
        stage_h.append(copy)
        sent.append(copy)

    def finish(s):
        stage_h[s].wait_recv()
        for jj in range(4):
            out[s, jj] = (own_h[s, jj] + recv_h[s, jj].astype(F32)) * scale

    for s in range(STEPS):
        for copy in over[s]:
            copy.wait_recv()

        def split(f, _, s=s):
            for q in range(KQ):
                re = src[s, q, f, :, :QB].astype(F32)
                im = src[s, q, f, :, QB:].astype(F32)
                at = (f, slice(None), pl.ds(q * QB, QB))
                s3[(0,) + at] = re
                s3[(1,) + at] = im
                s3[(2,) + at] = re - im
            return 0

        lax.fori_loop(0, NZ, split, 0)

        def cross(kt, _):
            at = pl.ds(pl.multiple_of(kt * 128, 128), 128)
            im_at = pl.ds(pl.multiple_of(HALF + kt * 128, 128), 128)
            for first_j in range(0, SB, 2):
                sums = [[jnp.zeros((2 * SB, 128), F32) for _ in range(3)] for _ in range(2)]
                for f in range(NZ):
                    r = [r3[c, f, :, at] for c in range(3)]
                    for n in range(2):
                        j = first_j + n
                        for c in range(3):
                            sums[n][c] = sums[n][c] + s3[c, f, j : j + 1, at] * r[c]
                for n in range(2):
                    j = first_j + n
                    a, b, c = sums[n]
                    row = ((j // 4) % 2 * 2 + j // 8) * 4 + j % 4
                    z[row * 32 : row * 32 + 32, at] = (a + b).astype(BF16)
                    z[row * 32 : row * 32 + 32, im_at] = (c - a + b).astype(BF16)
            return 0

        lax.fori_loop(0, HALF // 128, cross, 0)

        def to_lags(n, _):
            both = jnp.dot(z[...], lag[n], preferred_element_type=F32)
            both = both + jnp.dot(z[...], lag[n + 2], preferred_element_type=F32)
            both = both * keep
            lf[:, :, :, :, pl.ds(pl.multiple_of(n * 256, 256), 256)] = both.reshape(2, 8, 2, SB, 256)
            return 0

        lax.fori_loop(0, 2, to_lags, 0)
        if s >= 1:
            to_x(s - 1)

        def part(b, _, s=s):
            for xc in range(2):
                send_c[s, b // 4, b % 4, xc] = lf[1 - pc, b, xc].astype(BF16)
                own_c[b, xc] = lf[pc, b, xc]
            return 0

        lax.fori_loop(0, 8, part, 0)
        copy = remote(send_c.at[s], recv_c.at[s], rs_s.at[0, s], rs_r.at[0, s], dev_c)
        copy.start()
        stage_c.append(copy)
        sent.append(copy)
        if s >= 2:
            to_h(s - 2)
        if s >= 3:
            finish(s - 3)
    last = STEPS - 1
    to_x(last)
    to_h(last - 1)
    finish(last - 2)
    to_h(last)
    finish(last - 1)
    finish(last)
    for copy in sent:
        copy.wait_send()


def local(traces, valid_flags, source_block):
    vmem = lambda *shape, dtype=BF16: pltpu.VMEM(shape, dtype)
    dma = lambda *shape: pltpu.SemaphoreType.DMA(shape)
    return pl.pallas_call(
        kernel,
        out_shape=jax.ShapeDtypeStruct((STEPS, 4, SB, LAGS), F32),
        in_specs=[
            pl.BlockSpec(memory_space=pltpu.VMEM),
            pl.BlockSpec(memory_space=pltpu.SMEM),
            pl.BlockSpec(memory_space=pltpu.SMEM),
            pl.BlockSpec(memory_space=pl.ANY),
            pl.BlockSpec(memory_space=pl.ANY),
        ],
        out_specs=pl.BlockSpec(memory_space=pltpu.VMEM),
        scratch_shapes=[
            vmem(KQ, NFFT, QL),
            vmem(4, NFFT, LAGS // 2),
            vmem(KQ, 256, QL, dtype=F32),
            vmem(2, KQ, NZ, SB, QL),
            vmem(2 * NY, NZ, SB, QL),
            vmem(KQ, NZ, SB, QL),
            vmem(NZ, STEPS, SB, QL),
            *[vmem(NZ, SB, QL) for _ in range(STEPS)],
            vmem(STEPS, KQ, NZ, SB, QL),
            vmem(3, NZ, 2 * SB, HALF, dtype=F32),
            vmem(3, NZ, SB, HALF, dtype=F32),
            vmem(2 * SB * SB, NFFT),
            vmem(2, 8, 2, SB, LAGS, dtype=F32),
            vmem(STEPS, 2, 4, 2, SB, LAGS),
            vmem(STEPS, 2, 4, 2, SB, LAGS),
            vmem(STEPS, 2, 4, SB, LAGS),
            vmem(STEPS, 2, 4, SB, LAGS),
            vmem(STEPS, 4, SB, LAGS),
            vmem(STEPS, 4, SB, LAGS),
            vmem(8, 2, SB, LAGS, dtype=F32),
            vmem(STEPS, 2, 4, SB, LAGS, dtype=F32),
            vmem(STEPS, 4, SB, LAGS, dtype=F32),
            dma(KQ + 1),
            dma(7), dma(7), dma(2),
            dma(STEPS, NZ), dma(STEPS, NZ),
            dma(STEPS, NZ), dma(STEPS, NZ),
            dma(STEPS, NY), dma(STEPS, NY),
            dma(3, STEPS), dma(3, STEPS),
        ],
        compiler_params=pltpu.CompilerParams(
            collective_id=0, has_side_effects=True, vmem_limit_bytes=56 * 2**20
        ),
        name="correlate",
    )(traces, valid_flags, source_block, jnp.asarray(dft_table()), jnp.asarray(lag_table()))


def solution(mesh):
    placed = (P("seg", None, "rcv", None), P(), P())
    return jax.shard_map(
        local, mesh=mesh, in_specs=placed, out_specs=P(None, "seg", "rcv", None), check_vma=False
    )
```

time: 1050 us -> 104 us (0.10)
  waiting for transfers between devices: 590 us -> 0 us
  other arithmetic: 339 us -> 0 us
  Pallas kernels: 0 us -> 102 us
  starting transfers between devices: 65.2 us -> 0 us
  matrix products: 23.3 us -> 0 us
  between operations: 16.8 us -> 0.01 us
    psum x1 -> x0, waiting for transfers between devices: 566 us -> none  [spread(): return lax.psum(block, axis)]
    add x67 -> x0, other arithmetic: 207 us -> none  [the longest x64 207 us: add_row(): imag_acc = imag_acc + (s_real * r_imag - s_imag * r_real)]
    pallas_call x0 -> x1, Pallas kernels: none -> 102 us  [local(): pl.pallas_call(kernel, out_shape=jax.ShapeDtypeStruct((STEPS, 4, SB, LAGS...]
    all_to_all x4 -> x0, starting transfers between devices: 65.2 us -> none  [local(): lax.all_to_all(grouped, 'seg', split_axis=0, concat_axis=1, tiled=True)]
    convert_element_type x67 -> x0, other arithmetic: 57.3 us -> none  [the longest x64 56.9 us: add_row(): lax.dynamic_index_in_dim(rcv_rows, index, 0, False).astype(jnp.float32)]
    another operation x3 -> x0, other arithmetic: 35.8 us -> none
    all_to_all x4 -> x0, waiting for transfers between devices: 24 us -> none  [local(): lax.all_to_all(grouped, 'seg', split_axis=0, concat_axis=1, tiled=True)]
    dot_general x6 -> x0, matrix products: 23.3 us -> none  [the longest x4 14 us: local(): jnp.dot(stack.reshape(-1, length), lagtab, precision=lax.Precision.HIGHES...]
  transfers between devices with their start and end apart: 5 -> 0, of which waited for: 4 -> 0; matrix products, arithmetic and copies ran while one was open for 22% -> 0% of each run, Pallas kernels for 0% -> 0%
where the time goes in v1:
time: 104 us
  Pallas kernels  102 us (98%)
  local copies, waits for them, and re-layouts  1.88 us (2%)
    pallas_call x1, Pallas kernels, local(): pl.pallas_call(kernel, out_shape=jax.ShapeDtypeStruct((STEPS, 4, SB, LAGS...  102 us

profile of v1, /device:TPU:1, one launch (start us, length us, event | category | flops | bytes accessed | tf_op | source)
XLA Modules:
  0.0 104.3 jit_solution(6633104578760904843)
XLA Ops:
  0.0 102.4 %correlate.1 = f32[4,4,16,512]{3,2,1,0:T(8,128)} custom-call(bf16[2,8,16,2048]{3,2,1,0:T(8,128)(2,1)} %x_ref.1, s32[8]{0:T(128)} %flags.1, s32[4]{0:T(128)} %blocks.1, bf16[4,2048,512]{2,1,0:T(8,128)(2,1)} %constant.4.clone.tab_hbm, bf16[4,2048,256]{2,1,0:T(8,128)(2,1)} %constant.5.clone.lag_hbm), custom_call_target="tpu_custom_call" | custom-call | tf_op jit(solution)/shard_map/correlate/pallas_call | solution.py:290
  102.4 1.9 %copy.7 = f32[4,4,16,512]{3,2,1,0:T(8,128)} copy(f32[4,4,16,512]{3,2,1,0:T(8,128)} %correlate.1) | data formatting | bytes 1048576

commit v2 on v1

v2 whole, which is shorter than its diff:
```python
import math

import jax
import jax.numpy as jnp
import ml_dtypes
import numpy as np
from jax import lax
from jax.experimental import pallas as pl
from jax.experimental.pallas import tpu as pltpu
from jax.sharding import PartitionSpec as P

MESH = pl.DeviceIdType.MESH
NFFT = 2048
HALF = NFFT // 2
LAGS = 512
SB = 16
STEPS = 4
NY, NZ = 4, 8
KQ = 4
PB = HALF // KQ // 2
PL = 2 * PB
QL = 2 * PL
GROUPS = [(0, 0, 2), (0, 2, 2), (1, 0, 1), (1, 1, 1), (1, 2, 1), (1, 3, 1)]
F32, BF16 = jnp.float32, jnp.bfloat16


def dft_table():
    t = np.arange(NFFT)[:, None]
    k = np.arange(HALF)[None, :]
    angle = ((t * k) % NFFT) * (2.0 * math.pi / NFFT)
    both = np.stack([np.cos(angle), -np.sin(angle)], 1).reshape(NFFT, 2, KQ, 2, PB)
    return both.transpose(2, 0, 3, 1, 4).reshape(KQ, NFFT, QL).astype(ml_dtypes.bfloat16)


def lag_table():
    k = np.arange(HALF)[:, None]
    tau = np.arange(LAGS)[None, :] - LAGS // 2 + NFFT
    angle = ((k * tau) % NFFT) * (2.0 * math.pi / NFFT)
    full = np.stack([np.cos(angle), -np.sin(angle)], 0).reshape(2, 2 * KQ, PB, LAGS)
    return full.transpose(1, 0, 2, 3).reshape(NFFT, LAGS).astype(ml_dtypes.bfloat16)


def kernel(
    x_ref, flags, blocks, tab_hbm, lag_hbm, out,
    tab, lag, spec, w, rb1a, rb1b, rp, cand, rb20, rb21, rb22, rb23, rb24, rb25, src, r3, s3, z,
    send_c, recv_c, send_d, recv_d, own_c, own_d,
    tab_sem, a1_s, a1_r, rx_sem, az_s, az_r, gz_s, gz_r, gy_s, gy_r, rs_s, rs_r,
):
    rb1 = (rb1a, rb1b)
    rb2 = (rb20, rb21, rb22, rb23, rb24, rb25)
    rcv, seg = lax.axis_index("rcv"), lax.axis_index("seg")
    px, py, pz = rcv // 32, (rcv // 8) % 4, rcv % 8
    ph, pc = seg // 2, seg % 2
    me_q = px * NY + py

    def at_xy(dx, dy):
        return (px + dx) % 2, (py + dy) % NY

    def dev_xy(dx, dy):
        tx, ty = at_xy(dx, dy)
        return (tx * 32 + ty * 8 + pz, seg)

    def dev_z(dz):
        return (px * 32 + py * 8 + (pz + dz) % NZ, seg)

    dev_c = (rcv, ph * 2 + 1 - pc)

    def dev_far(dh, dx):
        return (((px + dx) % 2) * 32 + py * 8 + pz, ((ph + dh) % 2) * 2 + pc)

    plane = [(dx, dy) for dx in (0, 1) for dy in range(NY) if dx or dy]

    barrier = pltpu.get_barrier_semaphore()
    peers = [dev_xy(*d) for d in plane] + [dev_z(d) for d in range(1, NZ)] + [dev_c, dev_far(1, 0), dev_far(1, 1)]
    for peer in peers:
        pl.semaphore_signal(barrier, inc=1, device_id=peer, device_id_type=MESH)

    loads = [pltpu.make_async_copy(tab_hbm.at[q], tab.at[q], tab_sem.at[q]) for q in range(KQ)]
    loads.append(pltpu.make_async_copy(lag_hbm, lag, tab_sem.at[KQ]))
    for load in loads[:KQ]:
        load.start()

    def remote(a, b, s, r, peer):
        return pltpu.make_async_remote_copy(
            src_ref=a, dst_ref=b, send_sem=s, recv_sem=r, device_id=peer, device_id_type=MESH
        )

    rows = x_ref[...].reshape(256, NFFT)
    for q in range(KQ):
        loads[q].wait()
        spec[q] = jnp.dot(rows, tab[q], preferred_element_type=F32)

    loads[KQ].start()

    def whiten(row, _):
        at = pl.ds(pl.multiple_of(row * SB, SB), SB)
        parts = [spec[q, at, h * PL : h * PL + PL] for q in range(KQ) for h in range(2)]
        powers = [p[:, :PB] * p[:, :PB] + p[:, PB:] * p[:, PB:] for p in parts]
        total = jnp.sum(sum(powers), axis=-1, keepdims=True)
        level = 0.25 * (total * (1.0 / HALF)) + 1e-06
        for i, (part, power) in enumerate(zip(parts, powers)):
            factor = lax.rsqrt(power + level)
            w[row // 8, i % 2, i // 2, row % 8] = (part * jnp.concatenate([factor, factor], -1)).astype(BF16)
        return 0

    lax.fori_loop(0, 16, whiten, 0)

    pl.semaphore_wait(barrier, len(peers))

    sent = []
    first = [[], []]
    for h in range(2):
        for i, (dx, dy) in enumerate(plane):
            tx, ty = at_xy(dx, dy)
            first[h].append(
                remote(w.at[tx, h, ty], rb1[h].at[me_q], a1_s.at[h, i], a1_r.at[h, i], dev_xy(dx, dy))
            )
    swap = remote(w.at[1 - px], rp, rx_sem.at[0], rx_sem.at[1], dev_xy(1, 0))

    def fill(ref, row):
        def one(f, _):
            for q in range(KQ):
                for h in range(2):
                    re = ref[h, q, f, :, :PB].astype(F32)
                    im = ref[h, q, f, :, PB:].astype(F32)
                    lanes = pl.ds((q * 2 + h) * PB, PB)
                    at = (f, pl.ds(pl.multiple_of(row * SB, SB), SB), lanes)
                    r3[(0,) + at] = re
                    r3[(1,) + at] = im
                    r3[(2,) + at] = re + im
            return 0

        lax.fori_loop(0, NZ, one, 0)

    def choose(h):
        rb1[h][me_q] = w[px, h, py]
        for copy in first[h]:
            copy.wait_recv()
        for s in range(STEPS):
            cand[h, :, s] = rb1[h][blocks[s] // NZ]

    across, along, over = {}, {}, {}

    def send_across(g):
        h, s0, n = GROUPS[g]
        rb2[g][pz] = cand[h, pz, s0 : s0 + n]
        across[g] = []
        for dz in range(1, NZ):
            here = cand.at[h, (pz + dz) % NZ, pl.ds(s0, n)]
            copy = remote(here, rb2[g].at[pz], az_s.at[g, dz], az_r.at[g, dz], dev_z(dz))
            copy.start()
            across[g].append(copy)
        sent.extend(across[g])

    def send_along(g):
        h, s0, n = GROUPS[g]
        for copy in across[g]:
            copy.wait_recv()
        for i in range(n):
            src[h, s0 + i, py, pz] = rb2[g][blocks[s0 + i] % NZ, i]
        along[g] = []
        here = src.at[h, pl.ds(s0, n), py, pz]
        for dz in range(1, NZ):
            copy = remote(here, here, gz_s.at[g, dz], gz_r.at[g, dz], dev_z(dz))
            copy.start()
            along[g].append(copy)
        sent.extend(along[g])

    def send_over(g):
        h, s0, n = GROUPS[g]
        for copy in along[g]:
            copy.wait_recv()
        over[g] = []
        here = src.at[h, pl.ds(s0, n), py]
        for dy in (1, 3, 2):
            copy = remote(here, here, gy_s.at[g, dy], gy_r.at[g, dy], dev_xy(0, dy))
            copy.start()
            over[g].append(copy)
        sent.extend(over[g])

    def unit(h, s, q):
        def split(f, _):
            re = src[h, s, q, f, :, :PB].astype(F32)
            im = src[h, s, q, f, :, PB:].astype(F32)
            s3[0, f] = re
            s3[1, f] = im
            s3[2, f] = re - im
            return 0

        lax.fori_loop(0, NZ, split, 0)
        at = pl.ds(pl.multiple_of((q * 2 + h) * PB, PB), PB)
        re_at = pl.ds(pl.multiple_of((q * 2 + h) * PL, PL), PB)
        im_at = pl.ds(pl.multiple_of((q * 2 + h) * PL + PB, PB), PB)
        for xc in range(2):
            for first_j in range(0, SB, 4):
                sums = [[None] * 3 for _ in range(4)]
                for f in range(NZ):
                    for c in range(3):
                        r = r3[c, f, xc * SB : xc * SB + SB, at]
                        for n in range(4):
                            j = first_j + n
                            term = s3[c, f, j : j + 1, :] * r
                            sums[n][c] = term if f == 0 else sums[n][c] + term
                for n in range(4):
                    j = first_j + n
                    a, b, c = sums[n]
                    row = (((j // 4) % 2 * 2 + j // 8) * 4 + j % 4) * 32 + xc * SB
                    z[s, row : row + SB, re_at] = (a + b).astype(BF16)
                    z[s, row : row + SB, im_at] = (c - a + b).astype(BF16)

    def own_units(h, s0, n):
        def one(i, _):
            unit(h, s0 + i, py)
            return 0

        lax.fori_loop(0, n, one, 0)

    def other_units(g):
        h, s0, n = GROUPS[g]
        for copy in over[g]:
            copy.wait_recv()

        def one(i, _):
            unit(h, s0 + i // 3, (py + 1 + i % 3) % NY)
            return 0

        lax.fori_loop(0, 3 * n, one, 0)

    for copy in first[0]:
        copy.start()
    fill(w.at[px], px)
    for copy in first[0]:
        copy.wait_send()
    for copy in first[1]:
        copy.start()
    sent += first[1]
    choose(0)
    send_across(0)
    send_across(1)
    choose(1)
    swap.start()
    sent.append(swap)
    send_along(0)
    send_along(1)
    for g in range(2, 6):
        send_across(g)
    send_over(0)
    send_over(1)
    for g in range(2, 6):
        send_along(g)
    swap.wait_recv()
    fill(rp, 1 - px)
    own_units(0, 0, STEPS)
    for g in range(2, 6):
        send_over(g)
        own_units(1, g - 2, 1)
    loads[KQ].wait()

    count = flags[0]
    for g in range(1, 8):
        count = count + flags[g]
    scale = 1.0 / jnp.sqrt(jnp.full((SB, LAGS), HALF, F32) * (8 * count).astype(F32))
    keep = flags[seg * 2 + px].astype(F32)

    stage_c, stage_d = [], []
    others = [(0, 1), (1, 0), (1, 1)]

    def to_chips(s):
        stage_c[s].wait_recv()

        def one(b, _):
            for xc in range(2):
                both = own_c[s, b, xc] + recv_c[s, b // 4, b % 4, xc].astype(F32)
                own_d[s, b // 4, xc, b % 4] = both
                send_d[s, b // 4, xc, b % 4] = both.astype(BF16)
            return 0

        lax.fori_loop(0, 8, one, 0)
        group = []
        for i, (dh, dx) in enumerate(others):
            copy = remote(
                send_d.at[s, (ph + dh) % 2, (px + dx) % 2], recv_d.at[s, i],
                rs_s.at[1 + i, s], rs_r.at[1 + i, s], dev_far(dh, dx),
            )
            copy.start()
            group.append(copy)
        stage_d.append(group)
        sent.extend(group)

    def finish(s):
        for copy in stage_d[s]:
            copy.wait_recv()
        for jj in range(4):
            total = own_d[s, ph, px, jj]
            for i in range(3):
                total = total + recv_d[s, i, jj].astype(F32)
            out[s, jj] = total * scale

    for s in range(STEPS):
        if s == 0:
            other_units(0)
            other_units(1)
        other_units(2 + s)
        for own in (False, True):
            half = pc if own else 1 - pc
            rows = z[s, pl.ds(pl.multiple_of(half * 256, 256), 256), :]
            lags = jnp.dot(rows, lag[...], preferred_element_type=F32) * keep
            if own:
                own_c[s] = lags.reshape(8, 2, SB, LAGS)
            else:
                send_c[s] = lags.astype(BF16).reshape(2, 4, 2, SB, LAGS)
                copy = remote(send_c.at[s], recv_c.at[s], rs_s.at[0, s], rs_r.at[0, s], dev_c)
                copy.start()
                stage_c.append(copy)
                sent.append(copy)
        if s >= 1:
            to_chips(s - 1)

        if s >= 2:
            finish(s - 2)
    last = STEPS - 1
    to_chips(last)
    finish(last - 1)
    finish(last)
    for copy in sent:
        copy.wait_send()


def local(traces, valid_flags, source_block):
    vmem = lambda *shape, dtype=BF16: pltpu.VMEM(shape, dtype)
    dma = lambda *shape: pltpu.SemaphoreType.DMA(shape)
    return pl.pallas_call(
        kernel,
        out_shape=jax.ShapeDtypeStruct((STEPS, 4, SB, LAGS), F32),
        in_specs=[
            pl.BlockSpec(memory_space=pltpu.VMEM),
            pl.BlockSpec(memory_space=pltpu.SMEM),
            pl.BlockSpec(memory_space=pltpu.SMEM),
            pl.BlockSpec(memory_space=pl.ANY),
            pl.BlockSpec(memory_space=pl.ANY),
        ],
        out_specs=pl.BlockSpec(memory_space=pltpu.VMEM),
        scratch_shapes=[
            vmem(KQ, NFFT, QL),
            vmem(NFFT, LAGS),
            vmem(KQ, 256, QL, dtype=F32),
            vmem(2, 2, KQ, NZ, SB, PL),
            vmem(2 * NY, NZ, SB, PL),
            vmem(2 * NY, NZ, SB, PL),
            vmem(2, KQ, NZ, SB, PL),
            vmem(2, NZ, STEPS, SB, PL),
            *[vmem(NZ, n, SB, PL) for _, _, n in GROUPS],
            vmem(2, STEPS, KQ, NZ, SB, PL),
            vmem(3, NZ, 2 * SB, HALF, dtype=F32),
            vmem(3, NZ, SB, PB, dtype=F32),
            vmem(STEPS, 2 * SB * SB, NFFT),
            vmem(STEPS, 2, 4, 2, SB, LAGS),
            vmem(STEPS, 2, 4, 2, SB, LAGS),
            vmem(STEPS, 2, 2, 4, SB, LAGS),
            vmem(STEPS, 3, 4, SB, LAGS),
            vmem(STEPS, 8, 2, SB, LAGS, dtype=F32),
            vmem(STEPS, 2, 2, 4, SB, LAGS, dtype=F32),
            dma(KQ + 1),
            dma(2, 7), dma(2, 7), dma(2),
            dma(6, NZ), dma(6, NZ),
            dma(6, NZ), dma(6, NZ),
            dma(6, NY), dma(6, NY),
            dma(4, STEPS), dma(4, STEPS),
        ],
        compiler_params=pltpu.CompilerParams(
            collective_id=0, has_side_effects=True, vmem_limit_bytes=56 * 2**20
        ),
        name="correlate",
    )(traces, valid_flags, source_block, jnp.asarray(dft_table()), jnp.asarray(lag_table()))


def solution(mesh):
    placed = (P("seg", None, "rcv", None), P(), P())
    return jax.shard_map(
        local, mesh=mesh, in_specs=placed, out_specs=P(None, "seg", "rcv", None), check_vma=False
    )
```

time: 104 us -> 83.8 us (0.81)
  Pallas kernels: 102 us -> 81.2 us
    pallas_call x1, Pallas kernels: 102 us -> 81.2 us  [local(): pl.pallas_call(kernel, out_shape=jax.ShapeDtypeStruct((STEPS, 4, SB, LAGS...]
where the time goes in v2:
time: 83.8 us; the launch traced here: 83.1 us
  Pallas kernels  81.2 us (97%)
  local copies, waits for them, and re-layouts  1.88 us (2%)
    pallas_call x1, Pallas kernels, local(): pl.pallas_call(kernel, out_shape=jax.ShapeDtypeStruct((STEPS, 4, SB, LAGS...  81.2 us
    unnamed x1, local copies, waits for them, and re-layouts  1.88 us

profile of v2, /device:TPU:1, one launch (start us, length us, event | category | flops | bytes accessed | tf_op | source)
XLA Modules:
  0.0 83.1 jit_solution(14817779046736128876)
XLA Ops:
  0.0 81.2 %correlate.1 = f32[4,4,16,512]{3,2,1,0:T(8,128)} custom-call(bf16[2,8,16,2048]{3,2,1,0:T(8,128)(2,1)} %x_ref.1, s32[8]{0:T(128)} %flags.1, s32[4]{0:T(128)} %blocks.1, bf16[4,2048,512]{2,1,0:T(8,128)(2,1)} %constant.4.clone.tab_hbm, bf16[2048,512]{1,0:T(8,128)(2,1)} %constant.5.clone.lag_hbm), custom_call_target="tpu_custom_call" | custom-call | tf_op jit(solution)/shard_map/correlate/pallas_call | solution.py:332
  81.3 1.9 %copy.7 = f32[4,4,16,512]{3,2,1,0:T(8,128)} copy(f32[4,4,16,512]{3,2,1,0:T(8,128)} %correlate.1) | data formatting | bytes 1048576

commit v3 on v2

--- a/solution.py
+++ b/solution.py
@@ -42,7 +42,7 @@
 
 def kernel(
     x_ref, flags, blocks, tab_hbm, lag_hbm, out,
-    tab, lag, spec, w, rb1a, rb1b, rp, cand, rb20, rb21, rb22, rb23, rb24, rb25, src, r3, s3, z,
+    tab, lag, spec, w, rb1a, rb1b, rp, cand, rb20, rb21, rb22, rb23, rb24, rb25, src, r3, s3, z, lf,
     send_c, recv_c, send_d, recv_d, own_c, own_d,
     tab_sem, a1_s, a1_r, rx_sem, az_s, az_r, gz_s, gz_r, gy_s, gy_r, rs_s, rs_r,
 ):
@@ -233,25 +233,29 @@
         copy.wait_send()
     for copy in first[1]:
         copy.start()
-    sent += first[1]
     choose(0)
     send_across(0)
     send_across(1)
-    choose(1)
+    for copy in first[1]:
+        copy.wait_send()
     swap.start()
     sent.append(swap)
+    choose(1)
     send_along(0)
     send_along(1)
     for g in range(2, 6):
         send_across(g)
     send_over(0)
     send_over(1)
-    for g in range(2, 6):
-        send_along(g)
     swap.wait_recv()
     fill(rp, 1 - px)
     own_units(0, 0, STEPS)
     for g in range(2, 6):
+        send_along(g)
+    other_units(0)
+    for g in range(2, 6):
+        if g == 4:
+            other_units(1)
         send_over(g)
         own_units(1, g - 2, 1)
     loads[KQ].wait()
@@ -297,22 +301,15 @@
             out[s, jj] = total * scale
 
     for s in range(STEPS):
-        if s == 0:
-            other_units(0)
-            other_units(1)
         other_units(2 + s)
-        for own in (False, True):
-            half = pc if own else 1 - pc
-            rows = z[s, pl.ds(pl.multiple_of(half * 256, 256), 256), :]
-            lags = jnp.dot(rows, lag[...], preferred_element_type=F32) * keep
-            if own:
-                own_c[s] = lags.reshape(8, 2, SB, LAGS)
-            else:
-                send_c[s] = lags.astype(BF16).reshape(2, 4, 2, SB, LAGS)
-                copy = remote(send_c.at[s], recv_c.at[s], rs_s.at[0, s], rs_r.at[0, s], dev_c)
-                copy.start()
-                stage_c.append(copy)
-                sent.append(copy)
+        lags = jnp.dot(z[s], lag[...], preferred_element_type=F32) * keep
+        lf[...] = lags.reshape(2, 8, 2, SB, LAGS)
+        send_c[s] = lf[1 - pc].astype(BF16).reshape(2, 4, 2, SB, LAGS)
+        copy = remote(send_c.at[s], recv_c.at[s], rs_s.at[0, s], rs_r.at[0, s], dev_c)
+        copy.start()
+        stage_c.append(copy)
+        sent.append(copy)
+        own_c[s] = lf[pc]
         if s >= 1:
             to_chips(s - 1)
 
@@ -354,6 +351,7 @@
             vmem(3, NZ, 2 * SB, HALF, dtype=F32),
             vmem(3, NZ, SB, PB, dtype=F32),
             vmem(STEPS, 2 * SB * SB, NFFT),
+            vmem(2, 8, 2, SB, LAGS, dtype=F32),
             vmem(STEPS, 2, 4, 2, SB, LAGS),
             vmem(STEPS, 2, 4, 2, SB, LAGS),
             vmem(STEPS, 2, 2, 4, SB, LAGS),

time: 83.8 us -> 79.5 us (0.949)
  Pallas kernels: 81.2 us -> 77.4 us
    pallas_call x1, Pallas kernels: 81.2 us -> 77.4 us  [local(): pl.pallas_call(kernel, out_shape=jax.ShapeDtypeStruct((STEPS, 4, SB, LAGS...]
where the time goes in v3:
time: 79.5 us; the launch traced here: 79.3 us
  Pallas kernels  77.4 us (97%)
  local copies, waits for them, and re-layouts  1.88 us (2%)
    pallas_call x1, Pallas kernels, local(): pl.pallas_call(kernel, out_shape=jax.ShapeDtypeStruct((STEPS, 4, SB, LAGS...  77.4 us
    unnamed x1, local copies, waits for them, and re-layouts  1.88 us

profile of v3, /device:TPU:1, one launch (start us, length us, event | category | flops | bytes accessed | tf_op | source)
XLA Modules:
  0.0 79.3 jit_solution(17488788741654485946)
XLA Ops:
  0.0 77.4 %correlate.1 = f32[4,4,16,512]{3,2,1,0:T(8,128)} custom-call(bf16[2,8,16,2048]{3,2,1,0:T(8,128)(2,1)} %x_ref.1, s32[8]{0:T(128)} %flags.1, s32[4]{0:T(128)} %blocks.1, bf16[4,2048,512]{2,1,0:T(8,128)(2,1)} %constant.4.clone.tab_hbm, bf16[2048,512]{1,0:T(8,128)(2,1)} %constant.5.clone.lag_hbm), custom_call_target="tpu_custom_call" | custom-call | tf_op jit(solution)/shard_map/correlate/pallas_call | solution.py:329
  77.5 1.9 %copy.7 = f32[4,4,16,512]{3,2,1,0:T(8,128)} copy(f32[4,4,16,512]{3,2,1,0:T(8,128)} %correlate.1) | data formatting | bytes 1048576
